TPU v7x, 128 devices: a whole 4x4x4 slice. The times are simulated.
128 devices in a mesh: peer: 2 (over core), row: 16 (over y, x), col: 4 (over z).
Axes of the slice: x: 4, y: 4, z: 4, core: 2. Of those that a mesh axis runs over, the one named last changes fastest.
Arguments:
- block_in: bfloat16 [2, 768, 7168], P('peer', 'row', 'col'), may hold values from -6 to 6
- weight_in: bfloat16 [2, 7168, 14336], P('peer', 'col', 'row'), may hold values from -0.0625 to 0.0625
- weight_out: bfloat16 [2, 14336, 7168], P('peer', 'row', 'col'), may hold values from -0.046875 to 0.046875
- upstream: bfloat16 [2, 768, 7168], P('peer', 'row', 'col'), may hold values from -6 to 6
- stale_out: bfloat16 [2, 768, 7168], P('peer', 'row', 'col'), may hold values from -6 to 6
Outputs:
- block_out: bfloat16 [2, 768, 7168], P('peer', 'row', 'col')
- grad_block_in: bfloat16 [2, 768, 7168], P('peer', 'row', 'col')
- grad_weight_in: bfloat16 [2, 7168, 14336], P('peer', 'col', 'row')
- grad_weight_out: bfloat16 [2, 14336, 7168], P('peer', 'row', 'col')
All inputs are finite; a program needn't handle non-finite values.
Results may differ from a plain program's by a relative error of at most 0.024.
Values may be sent and summed in bfloat16 or wider, within the bound.
A program may use at most 128 MiB of HBM per device.

v0:
```python
import jax
import jax.numpy as jnp
from jax import lax
from jax.sharding import PartitionSpec as P

feature_weight = 1.0


def from_partner(x, axis, apart):
    return lax.ppermute(x, axis, [(i, i ^ 1 << apart) for i in range(lax.axis_size(axis))])


def gelu_value(values):
    return jax.nn.gelu(values, approximate=True)


def gelu_slope(values, cotangent):
    _, pull = jax.vjp(gelu_value, values)
    return pull(cotangent)[0]


def product(left, weight, flipped):
    if flipped:
        return lax.dot_general(
            left, weight, (((1,), (1,)), ((), ())), preferred_element_type=jnp.float32
        )
    return jnp.dot(left, weight, preferred_element_type=jnp.float32)


def gather_rows(block):
    return lax.all_gather(block, "row", axis=0, tiled=True)


def gather_cols(block):
    return lax.all_gather(block, "col", axis=0, tiled=True)


def reduce_cols(left, weight, flipped):
    share = left.shape[0] // lax.axis_size("col")

    def term(start, count):
        return product(left, weight, flipped)

    return lax.psum_scatter(
        term(jnp.int32(0), share * lax.axis_size("col")).astype(jnp.bfloat16),
        "col",
        scatter_dimension=0,
        tiled=True,
    ).astype(jnp.float32)


def reduce_rows(left, weight, flipped):
    share = left.shape[0] // lax.axis_size("row")

    def term(start, count):
        return product(left, weight, flipped)

    return lax.psum_scatter(
        term(jnp.int32(0), share * lax.axis_size("row")).astype(jnp.bfloat16),
        "row",
        scatter_dimension=0,
        tiled=True,
    ).astype(jnp.float32)


def body(block_in, weight_in, weight_out, upstream, stale_out):
    local_in = block_in[0]
    w_first = weight_in[0]
    w_second = weight_out[0]
    cotan = upstream[0]
    stale_other = from_partner(stale_out[0], "peer", 0)
    inputs_all = gather_rows(local_in)
    pre_local = reduce_cols(inputs_all, w_first, False)
    hidden_all = gather_cols(gelu_value(pre_local).astype(jnp.bfloat16))
    output = (local_in.astype(jnp.float32) + reduce_rows(hidden_all, w_second, False)).astype(
        jnp.bfloat16
    )
    slope_out = (
        cotan.astype(jnp.float32)
        + feature_weight * (output.astype(jnp.float32) - stale_other.astype(jnp.float32))
    ).astype(jnp.bfloat16)
    slope_all = gather_rows(slope_out)
    back_local = reduce_cols(slope_all, w_second, True)
    inner_all = gather_cols(gelu_slope(pre_local, back_local).astype(jnp.bfloat16))
    grad_in = (slope_out.astype(jnp.float32) + reduce_rows(inner_all, w_first, True)).astype(
        jnp.bfloat16
    )
    grad_first = lax.dot_general(
        inputs_all, inner_all, (((0,), (0,)), ((), ())), preferred_element_type=jnp.float32
    ).astype(jnp.bfloat16)
    grad_second = lax.dot_general(
        hidden_all, slope_all, (((0,), (0,)), ((), ())), preferred_element_type=jnp.float32
    ).astype(jnp.bfloat16)
    return (output[None], grad_in[None], grad_first[None], grad_second[None])


def solution(mesh):
    placed = (
        P("peer", "row", "col"),
        P("peer", "col", "row"),
        P("peer", "row", "col"),
        P("peer", "row", "col"),
        P("peer", "row", "col"),
    )
    return jax.shard_map(
        body,
        mesh=mesh,
        in_specs=placed,
        out_specs=(
            P("peer", "row", "col"),
            P("peer", "row", "col"),
            P("peer", "col", "row"),
            P("peer", "row", "col"),
        ),
        check_vma=False,
    )
```

profile of v0, /device:TPU:0, one launch (start us, length us, event | category | flops | bytes accessed | tf_op | source)
XLA Modules:
  0.0 397.3 jit_solution(3600644181391552592)
XLA Ops:
  7.2 0.0 copy-start
  7.2 0.0 all-gather.12.cloned.1.call-start
  7.2 0.7 all-gather.12.cloned.1.call-update
  7.9 0.0 reduce-scatter.5.cloned.1.call-start
  8.0 51.2 %all-gather.12.cloned.1.call-done = bf16[1,768,1792]{2,1,0:T(8,128)(2,1)} async-done(((bf16[1,48,1792]{2,1,0:T(8,128)(2,1)}), bf16[1,768,1792]{2,1,0:T(8,128)(2,1)}) %all-gather.12.cloned.1.call-update) | async-done | bytes 2752528 | tf_op jit(solution)/shard_map/all_gather | solution.py:31
  59.2 6.8 %fusion.10 = bf16[768,896]{1,0:T(8,128)(2,1)} fusion(bf16[1,1792,896]{2,1,0:T(8,128)(2,1)} %param.6, bf16[1,768,1792]{2,1,0:T(8,128)(2,1)} %all-gather.12.cloned.1.call-done), kind=kOutput, calls=%fused_computation.14 | convolution fusion | flops 2466938880 | bytes 7340032 | tf_op jit(solution)/shard_map/dot_general | solution.py:27
  66.0 0.0 reduce-scatter.5.cloned.1.call-update
  66.0 0.0 all-gather.6.cloned.1.call-start
  66.1 24.3 %reduce-scatter.5.cloned.1.call-done = bf16[192,896]{1,0:T(8,128)(2,1)} async-done(((bf16[768,896]{1,0:T(8,128)(2,1)}), bf16[192,896]{1,0:T(8,128)(2,1)}) %reduce-scatter.5.cloned.1.call-update) | async-done | bytes 344080 | tf_op jit(solution)/shard_map/reduce_scatter | solution.py:44
  90.4 1.9 fusion.26
  92.3 0.0 all-gather.6.cloned.1.call-update
  92.4 0.0 reduce-scatter.7.cloned.1.call-start
  92.4 25.4 %all-gather.6.cloned.1.call-done = bf16[768,896]{1,0:T(8,128)(2,1)} async-done(((bf16[192,896]{1,0:T(8,128)(2,1)}), bf16[768,896]{1,0:T(8,128)(2,1)}) %all-gather.6.cloned.1.call-update) | async-done | bytes 1376272 | tf_op jit(solution)/shard_map/all_gather | solution.py:35
  117.8 0.0 copy-done
  117.8 5.9 %convolution_convert_fusion.3 = bf16[768,1792]{1,0:T(8,128)(2,1)} fusion(bf16[768,896]{1,0:T(8,128)(2,1)} %all-gather.6.cloned.1.call-done, bf16[1,896,1792]{2,1,0:T(8,128)(2,1)S(1)} %copy-done), kind=kOutput, calls=%fused_computation.3 | convolution fusion | flops 2467627008 | bytes 7340032 | tf_op jit(solution)/shard_map/dot_general | solution.py:27
  123.7 0.0 reduce-scatter.7.cloned.1.call-update
  123.7 0.0 all-gather.8.cloned.1.call-start
  123.8 0.1 collective-permute-start
  123.9 1.7 collective-permute-done
  125.6 74.0 %reduce-scatter.7.cloned.1.call-done = bf16[48,1792]{1,0:T(8,128)(2,1)} async-done(((bf16[768,1792]{1,0:T(8,128)(2,1)}), bf16[48,1792]{1,0:T(8,128)(2,1)}) %reduce-scatter.7.cloned.1.call-update) | async-done | bytes 172048 | tf_op jit(solution)/shard_map/reduce_scatter | solution.py:58
  199.6 0.0 copy-done.3
  199.6 0.0 copy-done.4
  199.6 1.8 fusion.29
  201.5 0.0 all-gather.8.cloned.1.call-update
  201.5 0.0 copy-start.2
  201.5 0.0 reduce-scatter.9.cloned.1.call-start
  201.5 46.7 %all-gather.8.cloned.1.call-done = bf16[768,1792]{1,0:T(8,128)(2,1)} async-done(((bf16[48,1792]{1,0:T(8,128)(2,1)}), bf16[768,1792]{1,0:T(8,128)(2,1)}) %all-gather.8.cloned.1.call-update) | async-done | bytes 2752528 | tf_op jit(solution)/shard_map/all_gather | solution.py:31
  248.3 5.9 %fusion.15 = bf16[768,896]{1,0:T(8,128)(2,1)} fusion(bf16[768,1792]{1,0:T(8,128)(2,1)} %all-gather.8.cloned.1.call-done, bf16[1,896,1792]{2,1,0:T(8,128)(2,1)S(1)} %copy-done), kind=kOutput, calls=%fused_computation.15 | convolution fusion | flops 2466938880 | bytes 7340032 | tf_op jit(solution)/shard_map/dot_general | solution.py:24
  254.2 0.0 reduce-scatter.9.cloned.1.call-update
  254.2 0.0 all-gather.10.cloned.1.call-start
  254.2 24.3 %reduce-scatter.9.cloned.1.call-done = bf16[192,896]{1,0:T(8,128)(2,1)} async-done(((bf16[768,896]{1,0:T(8,128)(2,1)}), bf16[192,896]{1,0:T(8,128)(2,1)}) %reduce-scatter.9.cloned.1.call-update) | async-done | bytes 344080 | tf_op jit(solution)/shard_map/reduce_scatter | solution.py:44
  278.5 0.0 copy-done.2
  278.5 2.2 fusion.21
  280.8 0.0 all-gather.10.cloned.1.call-update
  280.8 0.2 reduce-scatter.11.cloned.1.call-start
  281.0 25.0 %all-gather.10.cloned.1.call-done = bf16[768,896]{1,0:T(8,128)(2,1)} async-done(((bf16[192,896]{1,0:T(8,128)(2,1)}), bf16[768,896]{1,0:T(8,128)(2,1)}) %all-gather.10.cloned.1.call-update) | async-done | bytes 1376272 | tf_op jit(solution)/shard_map/all_gather | solution.py:35
  306.0 6.9 %convolution_convert_fusion.2 = bf16[768,1792]{1,0:T(8,128)(2,1)} fusion(bf16[768,896]{1,0:T(8,128)(2,1)} %all-gather.10.cloned.1.call-done, bf16[1,1792,896]{2,1,0:T(8,128)(2,1)} %param.6), kind=kOutput, calls=%fused_computation.2 | convolution fusion | flops 2467627008 | bytes 7340032 | tf_op jit(solution)/shard_map/dot_general | solution.py:24
  312.9 0.0 reduce-scatter.11.cloned.1.call-update
  312.9 0.0 copy-start.5
  312.9 0.0 copy-start.6
  312.9 6.7 %fusion.7 = bf16[1,896,1792]{2,1,0:T(8,128)(2,1)} fusion(bf16[768,896]{1,0:T(8,128)(2,1)} %all-gather.6.cloned.1.call-done, bf16[768,1792]{1,0:T(8,128)(2,1)} %all-gather.8.cloned.1.call-done), kind=kOutput, calls=%fused_computation.11 | convolution fusion | flops 2467856384 | bytes 7340032 | tf_op jit(solution)/shard_map/dot_general | solution.py:91
  319.7 0.0 copy-done.5
  319.7 0.0 copy-done.6
  319.7 4.4 %fusion.6 = bf16[1,1792,896]{1,2,0:T(8,128)(2,1)} fusion(bf16[768,896]{1,0:T(8,128)(2,1)S(1)} %copy-done.6, bf16[1,768,1792]{2,1,0:T(8,128)(2,1)S(1)} %copy-done.5), kind=kOutput, calls=%fused_computation.10 | convolution fusion | flops 2467856384 | bytes 7340032 | tf_op jit(solution)/shard_map/dot_general | solution.py:88
  324.1 5.7 %copy.9 = bf16[1,1792,896]{2,1,0:T(8,128)(2,1)} copy(bf16[1,1792,896]{1,2,0:T(8,128)(2,1)} %fusion.6) | data formatting | bytes 6422528
  329.7 59.1 %reduce-scatter.11.cloned.1.call-done = bf16[48,1792]{1,0:T(8,128)(2,1)} async-done(((bf16[768,1792]{1,0:T(8,128)(2,1)}), bf16[48,1792]{1,0:T(8,128)(2,1)}) %reduce-scatter.11.cloned.1.call-update) | async-done | bytes 172048 | tf_op jit(solution)/shard_map/reduce_scatter | solution.py:58
  388.8 0.0 copy-done.1
  388.9 1.6 fusion.31
  (3 shorter events, 0.0 us)
Async XLA Ops:
  7.2 110.6 %copy-start = (bf16[1,896,1792]{2,1,0:T(8,128)(2,1)S(1)}, bf16[1,896,1792]{2,1,0:T(8,128)(2,1)}, u32[]{:S(2)}) copy-start(bf16[1,896,1792]{2,1,0:T(8,128)(2,1)} %param.7) | copy-start | bytes 9633796
  7.2 52.0 %all-gather.12.cloned.1.call-start = ((), (), s32[]{:S(2)}) async-start(), calls=%async_computation.11 | async-start | bytes 2924544 | tf_op jit(solution)/shard_map/all_gather | solution.py:31
  7.9 82.5 %reduce-scatter.5.cloned.1.call-start = ((), (), s32[]{:S(2)}) async-start(), calls=%async_computation.4 | async-start | bytes 1720320 | tf_op jit(solution)/shard_map/reduce_scatter | solution.py:44
  66.0 51.8 %all-gather.6.cloned.1.call-start = ((), (), s32[]{:S(2)}) async-start(), calls=%async_computation.5 | async-start | bytes 1720320 | tf_op jit(solution)/shard_map/all_gather | solution.py:35
  92.4 107.3 %reduce-scatter.7.cloned.1.call-start = ((), (), s32[]{:S(2)}) async-start(), calls=%async_computation.6 | async-start | bytes 2924544 | tf_op jit(solution)/shard_map/reduce_scatter | solution.py:58
  123.7 75.9 %copy-start.3 = (bf16[1,48,1792]{2,1,0:T(8,128)(2,1)S(1)}, bf16[1,48,1792]{2,1,0:T(8,128)(2,1)}, u32[]{:S(2)}) copy-start(bf16[1,48,1792]{2,1,0:T(8,128)(2,1)} %param.5) | copy-start | bytes 516100
  123.7 75.9 %copy-start.4 = (bf16[1,48,1792]{2,1,0:T(8,128)(2,1)S(1)}, bf16[1,48,1792]{2,1,0:T(8,128)(2,1)}, u32[]{:S(2)}) copy-start(bf16[1,48,1792]{2,1,0:T(8,128)(2,1)} %param.8) | copy-start | bytes 516100
  123.7 124.6 %all-gather.8.cloned.1.call-start = ((), (), s32[]{:S(2)}) async-start(), calls=%async_computation.7 | async-start | bytes 2924544 | tf_op jit(solution)/shard_map/all_gather | solution.py:31
  123.8 1.8 collective-permute-start
  201.5 77.0 %copy-start.2 = (bf16[192,896]{1,0:T(8,128)(2,1)S(1)}, bf16[192,896]{1,0:T(8,128)(2,1)}, u32[]{:S(2)}) copy-start(bf16[192,896]{1,0:T(8,128)(2,1)} %reduce-scatter.5.cloned.1.call-done) | copy-start | bytes 1032196
  201.5 77.0 %reduce-scatter.9.cloned.1.call-start = ((), (), s32[]{:S(2)}) async-start(), calls=%async_computation.8 | async-start | bytes 1720320 | tf_op jit(solution)/shard_map/reduce_scatter | solution.py:44
  254.2 51.8 %all-gather.10.cloned.1.call-start = ((), (), s32[]{:S(2)}) async-start(), calls=%async_computation.9 | async-start | bytes 1720320 | tf_op jit(solution)/shard_map/all_gather | solution.py:35
  280.8 108.1 %reduce-scatter.11.cloned.1.call-start = ((), (), s32[]{:S(2)}) async-start(), calls=%async_computation.10 | async-start | bytes 2924544 | tf_op jit(solution)/shard_map/reduce_scatter | solution.py:58
  312.9 6.8 %copy-start.5 = (bf16[1,768,1792]{2,1,0:T(8,128)(2,1)S(1)}, bf16[1,768,1792]{2,1,0:T(8,128)(2,1)}, u32[]{:S(2)}) copy-start(bf16[1,768,1792]{2,1,0:T(8,128)(2,1)} %all-gather.12.cloned.1.call-done) | copy-start | bytes 8257540
  312.9 6.8 %copy-start.6 = (bf16[768,896]{1,0:T(8,128)(2,1)S(1)}, bf16[768,896]{1,0:T(8,128)(2,1)}, u32[]{:S(2)}) copy-start(bf16[768,896]{1,0:T(8,128)(2,1)} %all-gather.10.cloned.1.call-done) | copy-start | bytes 4128772
  324.1 64.8 %copy-start.1 = (bf16[48,1792]{1,0:T(8,128)(2,1)S(1)}, bf16[48,1792]{1,0:T(8,128)(2,1)}, u32[]{:S(2)}) copy-start(bf16[48,1792]{1,0:T(8,128)(2,1)} %get-tuple-element.8) | copy-start | bytes 516100
Sparse Core Ops, SparseCore 0:
  10.2 48.9 all-gather.11
  66.1 24.1 reduce-scatter.4
  92.7 25.0 all-gather.5
  123.8 75.7 reduce-scatter.6
  202.4 45.8 all-gather.7
  254.3 24.1 reduce-scatter.8
  280.9 25.0 all-gather.9
  313.0 75.7 reduce-scatter.10
where the time goes:
time: 398 us; the launch traced here: 397 us
  waiting for transfers between devices  333 us (84%)
  matrix products  36.7 us (9%)
  between operations  14.2 us (4%)
  other arithmetic  7.62 us (2%)
  local copies, waits for them, and re-layouts  5.7 us (1%)
    reduce_scatter x2, waiting for transfers between devices, reduce_rows(): lax.psum_scatter(term(jnp.int32(0), share * lax.axis_size('row')).astype(...  133 us
    all_gather x2, waiting for transfers between devices, gather_rows(): return lax.all_gather(block, 'row', axis=0, tiled=True)  97.9 us
    all_gather x2, waiting for transfers between devices, gather_cols(): return lax.all_gather(block, 'col', axis=0, tiled=True)  50.4 us
    reduce_scatter x2, waiting for transfers between devices, reduce_cols(): lax.psum_scatter(term(jnp.int32(0), share * lax.axis_size('col')).astype(...  48.6 us
    dot_general x2, matrix products, product(): lax.dot_general(left, weight, (((1,), (1,)), ((), ())), preferred_element...  12.8 us
    dot_general x2, matrix products, product(): return jnp.dot(left, weight, preferred_element_type=jnp.float32)  12.7 us
  transfers between devices with their start and end apart: 9, of which 9 were waited for; matrix products, arithmetic and copies ran while one was open for 4% of the time, Pallas kernels for 0%

commit v1 on v0

v1 whole, which is shorter than its diff:
```python
import functools

import jax
import jax.numpy as jnp
from jax import lax
from jax.experimental import pallas as pl
from jax.experimental.pallas import tpu as pltpu
from jax.sharding import PartitionSpec as P

feature_weight = 1.0
SIDE = 4
CHUNKS = 3
LAG = 1
STEPS = 12
MESH = pl.DeviceIdType.MESH
F32 = jnp.float32
BF16 = jnp.bfloat16


def gelu_both(v):
    inner = 0.7978845608 * (v + 0.044715 * v * v * v)
    t = jnp.tanh(inner)
    half = 0.5 * (1.0 + t)
    value = v * half
    slope = half + 0.5 * v * (1.0 - t * t) * (0.7978845608 * (1.0 + 3.0 * 0.044715 * v * v))
    return value, slope


def column_tiles(width, run):
    full = width // 256

    def step(n, carry):
        run(pl.multiple_of(n * 256, 256), 256)
        return carry

    lax.fori_loop(0, full, step, 0)
    if width % 256:
        run(full * 256, width % 256)


def kernel(
    x_ref, g_ref, s_ref, w1_ref, w2_ref,
    out_ref, gin_ref, gw1_ref, gw2_ref,
    w1, w2, stale, x_all, slope_all, hidden_all, inner_all, dgelu,
    part1, part2, got_z1, got_z2, outp, ginp,
    big_a, big_b, sum_a, sum_b, small_a, small_b, gw1, gw2,
    send_sem, recv_sem, stale_sem, local_sem, out_sem,
):
    tokens = x_ref.shape[0] // CHUNKS
    wide, units = w1.shape
    half = wide // 2
    rows = tokens * SIDE * SIDE
    left, right = pl.ds(0, half), pl.ds(half, half)
    peer, row, z = lax.axis_index("peer"), lax.axis_index("row"), lax.axis_index("col")
    y, x = lax.div(row, SIDE), lax.rem(row, SIDE)

    def at(axis, d):
        if axis == "x":
            return lax.rem(x + d, SIDE)
        if axis == "y":
            return lax.rem(y + d, SIDE)
        return lax.rem(z + d, SIDE)

    def device(axis, d):
        if axis == "x":
            return (peer, y * SIDE + at("x", d), z)
        if axis == "y":
            return (peer, at("y", d) * SIDE + x, z)
        return (peer, row, at("z", d))

    other = (1 - peer, row, z)

    load1 = pltpu.make_async_copy(w1_ref, w1, local_sem.at[0])
    load2 = pltpu.make_async_copy(w2_ref, w2, local_sem.at[1])
    load1.start()
    load2.start()

    barrier = pltpu.get_barrier_semaphore()
    for axis in "xyz":
        for d in range(1, SIDE):
            pl.semaphore_signal(barrier, inc=1, device_id=device(axis, d), device_id_type=MESH)
    pl.semaphore_signal(barrier, inc=1, device_id=other, device_id_type=MESH)
    for k in range(CHUNKS):
        x_all[k, y, x] = x_ref[pl.ds(k * tokens, tokens), :]
    pl.semaphore_wait(barrier, 3 * (SIDE - 1) + 1)

    flights = {}

    def send(k, e, src, dst, target):
        held = flights.setdefault((k, e), [])
        copy = pltpu.make_async_remote_copy(
            src_ref=src,
            dst_ref=dst,
            send_sem=send_sem.at[k, e, len(held)],
            recv_sem=recv_sem.at[k, e, len(held)],
            device_id=target,
            device_id_type=MESH,
        )
        copy.start()
        held.append(copy)

    def arrive(k, e):
        for copy in flights[k, e]:
            copy.wait_recv()

    ring = range(1, SIDE)

    def gather_first(k, e, buf):
        for d in ring:
            send(k, e, buf.at[k, y, x, :, left], buf.at[k, y, x, :, left], device("x", d))
            send(k, e, buf.at[k, y, x, :, right], buf.at[k, y, x, :, right], device("y", d))

    def gather_second(k, e, buf):
        arrive(k, e - 1)
        for d in ring:
            send(k, e, buf.at[k, y, :, :, left], buf.at[k, y, :, :, left], device("y", d))
            send(k, e, buf.at[k, :, x, :, right], buf.at[k, :, x, :, right], device("x", d))

    def scatter_left(k, e, i, buf):
        for d in ring:
            send(k, e, buf.at[k, at("y", d), :, :, left], big_a.at[i, k, d - 1], device("y", d))

    def scatter_right(k, e, i, buf):
        for d in ring:
            send(k, e, buf.at[k, :, at("x", d), :, right], big_b.at[i, k, d - 1], device("x", d))

    def scatter_second(k, e, i, buf):
        arrive(k, e - 1)
        for n in range(SIDE):
            total = buf[k, y, n, :, left].astype(F32)
            for d in ring:
                total = total + big_a[i, k, d - 1, n].astype(F32)
            sum_a[i, k, n] = total.astype(BF16)
        for d in ring:
            send(k, e, sum_a.at[i, k, at("x", d)], small_a.at[i, k, d - 1], device("x", d))
        for n in range(SIDE):
            total = buf[k, n, x, :, right].astype(F32)
            for d in ring:
                total = total + big_b[i, k, d - 1, n].astype(F32)
            sum_b[i, k, n] = total.astype(BF16)
        for d in ring:
            send(k, e, sum_b.at[i, k, at("y", d)], small_b.at[i, k, d - 1], device("y", d))

    def scatter_total(k, e, i):
        arrive(k, e - 1)
        a = sum_a[i, k, x].astype(F32)
        b = sum_b[i, k, y].astype(F32)
        for d in ring:
            a = a + small_a[i, k, d - 1].astype(F32)
            b = b + small_b[i, k, d - 1].astype(F32)
        return (left, a), (right, b)

    def col_scatter(k, e, buf, got):
        for d in ring:
            send(k, e, buf.at[k, at("z", d)], got.at[k, d - 1], device("z", d))

    def col_total(k, e, buf, got):
        arrive(k, e - 1)
        total = buf[k, z].astype(F32)
        for d in ring:
            total = total + got[k, d - 1].astype(F32)
        return total

    def col_gather(k, e, buf):
        for d in ring:
            send(k, e, buf.at[k, z], buf.at[k, z], device("z", d))

    def to_units(k, src, weight, flipped, dst):
        def tile(start, size):
            block = src[k].reshape(rows, wide)
            if flipped:
                value = lax.dot_general(
                    block, weight[pl.ds(start, size), :], (((1,), (1,)), ((), ())),
                    preferred_element_type=F32,
                )
            else:
                value = jnp.dot(block, weight[:, pl.ds(start, size)], preferred_element_type=F32)
            dst[k, :, :, pl.ds(start, size)] = value.astype(BF16).reshape(SIDE, rows // SIDE, size)

        column_tiles(units, tile)

    def to_features(k, src, weight, flipped, dst, base):
        def tile(offset, size):
            start = base + offset
            if not isinstance(start, int):
                start = pl.multiple_of(start, 128)
            block = src[k].reshape(rows, units)
            if flipped:
                value = lax.dot_general(
                    block, weight[pl.ds(start, size), :], (((1,), (1,)), ((), ())),
                    preferred_element_type=F32,
                )
            else:
                value = jnp.dot(block, weight[:, pl.ds(start, size)], preferred_element_type=F32)
            dst[k, :, :, :, pl.ds(start, size)] = value.astype(BF16).reshape(
                SIDE, SIDE, tokens, size
            )

        column_tiles(half, tile)

    def local(k):
        return pl.ds(k * tokens, tokens)

    everyone = CHUNKS * rows

    def weight_gradient(narrow, other_all, result, width):
        def tile(start, size):
            a = narrow[..., pl.ds(start, size)].reshape(everyone, size)
            b = other_all[...].reshape(everyone, width)
            result[pl.ds(start, size), :] = lax.dot_general(
                a, b, (((0,), (0,)), ((), ())), preferred_element_type=F32
            ).astype(BF16)

        return tile

    def event(k, e):
        if e == 0:
            gather_first(k, e, x_all)
        elif e == 1:
            gather_second(k, e, x_all)
        elif e == 2:
            arrive(k, e - 1)
            if k == 0:
                load1.wait()
            to_units(k, x_all, w1, False, part1)
            col_scatter(k, e, part1, got_z1)
        elif e == 3:
            value, slope = gelu_both(col_total(k, e, part1, got_z1))
            hidden_all[k, z] = value.astype(BF16)
            col_gather(k, e, hidden_all)
            dgelu[k] = slope
        elif e == 4:
            arrive(k, e - 1)
            if k == 0:
                load2.wait()
            to_features(k, hidden_all, w2, False, outp, 0)
            scatter_left(k, e, 0, outp)
            to_features(k, hidden_all, w2, False, outp, half)
            scatter_right(k, e, 0, outp)
        elif e == 5:
            scatter_second(k, e, 0, outp)
        elif e == 6:
            if k == 0:
                swap.wait_recv()
            for cols, total in scatter_total(k, e, 0):
                output = (x_ref[local(k), cols].astype(F32) + total).astype(BF16)
                out_ref[local(k), cols] = output
                slope = g_ref[local(k), cols].astype(F32) + feature_weight * (
                    output.astype(F32) - stale[local(k), cols].astype(F32)
                )
                slope_all[k, y, x, :, cols] = slope.astype(BF16)
            gather_first(k, e, slope_all)
        elif e == 7:
            gather_second(k, e, slope_all)
        elif e == 8:
            arrive(k, e - 1)
            to_units(k, slope_all, w2, True, part2)
            col_scatter(k, e, part2, got_z2)
            if k == CHUNKS - 1:
                column_tiles(units, weight_gradient(hidden_all, slope_all, gw2, wide))
                save2.start()
        elif e == 9:
            inner = col_total(k, e, part2, got_z2) * dgelu[k]
            inner_all[k, z] = inner.astype(BF16)
            col_gather(k, e, inner_all)
        elif e == 10:
            arrive(k, e - 1)
            to_features(k, inner_all, w1, True, ginp, 0)
            scatter_left(k, e, 1, ginp)
            to_features(k, inner_all, w1, True, ginp, half)
            scatter_right(k, e, 1, ginp)
            if k == CHUNKS - 1:
                column_tiles(wide, weight_gradient(x_all, inner_all, gw1, units))
                save1.start()
        elif e == 11:
            scatter_second(k, e, 1, ginp)
        elif e == 12:
            for cols, total in scatter_total(k, e, 1):
                mine = slope_all[k, y, x, :, cols].astype(F32)
                gin_ref[local(k), cols] = (mine + total).astype(BF16)

    swap = pltpu.make_async_remote_copy(
        src_ref=s_ref, dst_ref=stale, send_sem=stale_sem.at[0], recv_sem=stale_sem.at[1],
        device_id=other, device_id_type=MESH,
    )
    save1 = pltpu.make_async_copy(gw1, gw1_ref, out_sem.at[0])
    save2 = pltpu.make_async_copy(gw2, gw2_ref, out_sem.at[1])

    for tick in range(STEPS + 1 + LAG * (CHUNKS - 1)):
        for k in range(CHUNKS):
            e = tick - LAG * k
            if 0 <= e <= STEPS:
                event(k, e)
        if tick == 0:
            swap.start()
    swap.wait_send()
    for held in flights.values():
        for copy in held:
            copy.wait_send()
    save2.wait()
    save1.wait()


def body(block_in, weight_in, weight_out, upstream, stale_out):
    x, w1, w2, g, s = block_in[0], weight_in[0], weight_out[0], upstream[0], stale_out[0]
    wide, units = w1.shape
    own = x.shape[0]
    tokens = own // CHUNKS
    rows = tokens * SIDE * SIDE
    half = wide // 2
    share = rows // SIDE
    ring = SIDE - 1
    inside = pl.BlockSpec(memory_space=pltpu.VMEM)
    anywhere = pl.BlockSpec(memory_space=pl.ANY)
    row_all = pltpu.VMEM((CHUNKS, SIDE, SIDE, tokens, wide), BF16)
    col_all = pltpu.VMEM((CHUNKS, SIDE, share, units), BF16)
    col_got = pltpu.VMEM((CHUNKS, ring, share, units), BF16)
    flops = 12 * own * 16 * wide * units
    out, gin, gw1, gw2 = pl.pallas_call(
        kernel,
        out_shape=(
            jax.ShapeDtypeStruct(x.shape, BF16),
            jax.ShapeDtypeStruct(x.shape, BF16),
            jax.ShapeDtypeStruct(w1.shape, BF16),
            jax.ShapeDtypeStruct(w2.shape, BF16),
        ),
        in_specs=[inside, inside, inside, anywhere, anywhere],
        out_specs=(inside, inside, anywhere, anywhere),
        scratch_shapes=[
            pltpu.VMEM((wide, units), BF16),
            pltpu.VMEM((units, wide), BF16),
            pltpu.VMEM(x.shape, BF16),
            row_all,
            row_all,
            col_all,
            col_all,
            pltpu.VMEM((CHUNKS, share, units), F32),
            col_all,
            col_all,
            col_got,
            col_got,
            row_all,
            row_all,
            pltpu.VMEM((2, CHUNKS, ring, SIDE, tokens, half), BF16),
            pltpu.VMEM((2, CHUNKS, ring, SIDE, tokens, half), BF16),
            pltpu.VMEM((2, CHUNKS, SIDE, tokens, half), BF16),
            pltpu.VMEM((2, CHUNKS, SIDE, tokens, half), BF16),
            pltpu.VMEM((2, CHUNKS, ring, tokens, half), BF16),
            pltpu.VMEM((2, CHUNKS, ring, tokens, half), BF16),
            pltpu.VMEM((wide, units), BF16),
            pltpu.VMEM((units, wide), BF16),
            pltpu.SemaphoreType.DMA((CHUNKS, STEPS, 2 * ring)),
            pltpu.SemaphoreType.DMA((CHUNKS, STEPS, 2 * ring)),
            pltpu.SemaphoreType.DMA((2,)),
            pltpu.SemaphoreType.DMA((2,)),
            pltpu.SemaphoreType.DMA((2,)),
        ],
        compiler_params=pltpu.CompilerParams(
            collective_id=0, has_side_effects=True, vmem_limit_bytes=60 << 20
        ),
        cost_estimate=pl.CostEstimate(
            flops=flops, bytes_accessed=8 * wide * units, transcendentals=0
        ),
    )(x, g, s, w1, w2)
    return out[None], gin[None], gw1[None], gw2[None]


def solution(mesh):
    placed = (
        P("peer", "row", "col"),
        P("peer", "col", "row"),
        P("peer", "row", "col"),
        P("peer", "row", "col"),
        P("peer", "row", "col"),
    )
    return jax.shard_map(
        body,
        mesh=mesh,
        in_specs=placed,
        out_specs=(
            P("peer", "row", "col"),
            P("peer", "row", "col"),
            P("peer", "col", "row"),
            P("peer", "row", "col"),
        ),
        check_vma=False,
    )
```

time: 398 us -> 139 us (0.35)
  waiting for transfers between devices: 333 us -> 0 us
  Pallas kernels: 0 us -> 129 us
  matrix products: 36.7 us -> 0 us
  between operations: 14.2 us -> 0.64 us
  other arithmetic: 7.62 us -> 0 us
    reduce_scatter x4 -> x0, waiting for transfers between devices: 182 us -> none  [the longest x2 133 us: reduce_rows(): lax.psum_scatter(term(jnp.int32(0), share * lax.axis_size('row')).astype(...]
    all_gather x4 -> x0, waiting for transfers between devices: 148 us -> none  [the longest x2 97.9 us: gather_rows(): return lax.all_gather(block, 'row', axis=0, tiled=True)]
    pallas_call x0 -> x1, Pallas kernels: none -> 129 us  [body(): pl.pallas_call(kernel, out_shape=(jax.ShapeDtypeStruct(x.shape, BF16), ja...]
    dot_general x6 -> x0, matrix products: 36.7 us -> none  [the longest x2 12.8 us: product(): lax.dot_general(left, weight, (((1,), (1,)), ((), ())), preferred_element...]
    convert_element_type x3 -> x0, other arithmetic: 5.99 us -> none  [the longest x1 2.22 us: body(): gelu_slope(pre_local, back_local).astype(jnp.bfloat16)]
    unnamed x15 -> x6, local copies, waits for them, and re-layouts: 5.7 us -> 8.88 us
  transfers between devices with their start and end apart: 9 -> 0, of which waited for: 9 -> 0; matrix products, arithmetic and copies ran while one was open for 4% -> 0% of each run, Pallas kernels for 0% -> 0%
where the time goes in v1:
time: 139 us
  Pallas kernels  129 us (93%)
  local copies, waits for them, and re-layouts  8.88 us (6%)
    pallas_call x1, Pallas kernels, body(): pl.pallas_call(kernel, out_shape=(jax.ShapeDtypeStruct(x.shape, BF16), ja...  129 us
    unnamed x6, local copies, waits for them, and re-layouts  8.88 us

profile of v1, /device:TPU:0, one launch (start us, length us, event | category | flops | bytes accessed | tf_op | source)
XLA Modules:
  0.0 138.8 jit_solution(13899572450626622238)
XLA Ops:
  0.6 129.2 %shard_map.84 = (bf16[48,1792]{1,0:T(8,128)(2,1)}, bf16[48,1792]{1,0:T(8,128)(2,1)}, bf16[1792,896]{1,0:T(8,128)(2,1)}, bf16[896,1792]{1,0:T(8,128)(2,1)}) custom-call(bf16[48,1792]{1,0:T(8,128)(2,1)} %bitcast.15, bf16[48,1792]{1,0:T(8,128)(2,1)} %bitcast.16, bf16[48,1792]{1,0:T(8,128)(2,1)} %bitcast.17, bf16[1792,896]{1,0:T(8,128)(2,1)} %bitcast.13, ...), custom_call_target="tpu_custom_call" | custom-call | flops 14797504512 | bytes 12845056 | tf_op jit(solution)/shard_map/pallas_call | solution.py:319
  129.9 1.6 %copy.13 = bf16[1,48,1792]{2,1,0:T(8,128)(2,1)} copy(bf16[1,48,1792]{2,1,0:T(8,128)(2,1)} %bitcast.12) | data formatting | bytes 344064
  131.5 1.6 %copy.14 = bf16[1,48,1792]{2,1,0:T(8,128)(2,1)} copy(bf16[1,48,1792]{2,1,0:T(8,128)(2,1)} %bitcast.11) | data formatting | bytes 344064
  133.1 0.0 copy-start
  133.1 4.0 %copy.15 = bf16[1,1792,896]{2,1,0:T(8,128)(2,1)} copy(bf16[1,1792,896]{2,1,0:T(8,128)(2,1)} %bitcast.10) | data formatting | bytes 6422528
  137.1 0.0 copy-done
  137.1 1.7 %copy.16 = bf16[1,896,1792]{2,1,0:T(8,128)(2,1)} copy(bf16[1,896,1792]{2,1,0:T(8,128)(2,1)S(1)} %bitcast.9) | data formatting | bytes 6422528
Async XLA Ops:
  133.1 4.0 %copy-start = (bf16[896,1792]{1,0:T(8,128)(2,1)S(1)}, bf16[896,1792]{1,0:T(8,128)(2,1)}, u32[]{:S(2)}) copy-start(bf16[896,1792]{1,0:T(8,128)(2,1)} %get-tuple-element.11) | copy-start | bytes 9633796

commit v2 on v1

v2 whole, which is shorter than its diff:
```python
import functools

import jax
import jax.numpy as jnp
from jax import lax
from jax.experimental import pallas as pl
from jax.experimental.pallas import tpu as pltpu
from jax.sharding import PartitionSpec as P

feature_weight = 1.0
SIDE = 4
CHUNKS = 3
CUTS = ((0, 512), (512, 384))
STEPS = 12
ORDER = (
    (0, 0, 1), (0, 0, 0), (1, 0, 1), (0, 1, 1), (1, 0, 0), (0, 1, 0), (1, 1, 0), (1, 1, 1),
    (0, 2, 0), (2, 0, 0), (2, 0, 1), (1, 2, 0), (2, 1, 1), (2, 1, 0), (0, 3, 1), (0, 3, 0),
    (1, 3, 1), (1, 3, 0), (0, 4, 0), (2, 2, 0), (1, 4, 0), (0, 5, 1), (2, 3, 1), (0, 5, 0),
    (1, 5, 0), (0, 6, 1), (0, 6, 0), (2, 3, 0), (1, 5, 1), (0, 7, 1), (0, 7, 0), (2, 4, 0),
    (0, 8, 0), (1, 6, 0), (1, 6, 1), (2, 5, 0), (2, 5, 1), (1, 7, 0), (0, 9, 0), (2, 6, 0),
    (1, 7, 1), (0, 9, 1), (2, 6, 1), (2, 7, 0), (2, 7, 1), (1, 8, 0), (0, 10, 0), (2, 8, 0),
    (1, 9, 0), (1, 9, 1), (0, 13, 0), (0, 11, 1), (0, 11, 0), (2, 9, 0), (2, 9, 1), (1, 10, 0),
    (0, 12, 0), (2, 10, 0), (0, 14, 0), (1, 11, 0), (1, 11, 1), (2, 11, 0), (2, 11, 1), (0, 12, 1),
    (2, 12, 0), (1, 12, 0), (1, 12, 1), (2, 12, 1),
)
MESH = pl.DeviceIdType.MESH
F32 = jnp.float32
BF16 = jnp.bfloat16


def gelu_both(v):
    inner = 0.7978845608 * (v + 0.044715 * v * v * v)
    t = jnp.tanh(inner)
    half = 0.5 * (1.0 + t)
    value = v * half
    slope = half + 0.5 * v * (1.0 - t * t) * (0.7978845608 * (1.0 + 3.0 * 0.044715 * v * v))
    return value, slope


def column_tiles(width, run):
    full = width // 256

    def step(n, carry):
        run(pl.multiple_of(n * 256, 256), 256)
        return carry

    lax.fori_loop(0, full, step, 0)
    if width % 256:
        run(full * 256, width % 256)


def kernel(
    x_ref, g_ref, s_ref, w1_ref, w2_ref,
    out_ref, gin_ref, gw1_ref, gw2_ref,
    w1, w2, stale, x_all, slope_all, hidden_all, inner_all, dgelu,
    part1, part2, got_z1, got_z2, outp, ginp,
    big, small, sum_a, sum_b, gw1, gw2,
    send_sem, recv_sem, stale_sem, local_sem, out_sem,
):
    tokens = x_ref.shape[0] // CHUNKS
    wide, units = w1.shape
    half = wide // 2
    rows = tokens * SIDE * SIDE
    peer, row, z = lax.axis_index("peer"), lax.axis_index("row"), lax.axis_index("col")
    y, x = lax.div(row, SIDE), lax.rem(row, SIDE)

    def at(axis, d):
        if axis == "x":
            return lax.rem(x + d, SIDE)
        if axis == "y":
            return lax.rem(y + d, SIDE)
        return lax.rem(z + d, SIDE)

    def device(axis, d):
        if axis == "x":
            return (peer, y * SIDE + at("x", d), z)
        if axis == "y":
            return (peer, at("y", d) * SIDE + x, z)
        return (peer, row, at("z", d))

    other = (1 - peer, row, z)

    load1 = pltpu.make_async_copy(w1_ref, w1, local_sem.at[0])
    load2 = pltpu.make_async_copy(w2_ref, w2, local_sem.at[1])
    load1.start()
    load2.start()

    barrier = pltpu.get_barrier_semaphore()
    for axis in "xyz":
        for d in range(1, SIDE):
            pl.semaphore_signal(barrier, inc=1, device_id=device(axis, d), device_id_type=MESH)
    pl.semaphore_signal(barrier, inc=1, device_id=other, device_id_type=MESH)
    for k in range(CHUNKS):
        x_all[k, y, x] = x_ref[pl.ds(k * tokens, tokens), :]
    pl.semaphore_wait(barrier, 3 * (SIDE - 1) + 1)

    def send(key, src, dst, target):
        copy = pltpu.make_async_remote_copy(
            src_ref=src,
            dst_ref=dst,
            send_sem=send_sem.at[key],
            recv_sem=recv_sem.at[key],
            device_id=target,
            device_id_type=MESH,
        )
        copy.start()

    def bytes_of(e, g):
        cols = pl.ds(*CUTS[g])
        if e in (2, 3, 8, 9):
            return got_z1.at[0, :, :, cols]
        if e in (0, 5, 6, 11):
            return small.at[0, 0, :, :, :, cols]
        return big.at[0, 0, :, :, :, :, cols]

    def arrive(k, e, g):
        held = bytes_of(e, g)
        pltpu.make_async_copy(held, held, recv_sem.at[k, e, g]).wait()

    def leave(k, e, g):
        held = bytes_of(e, g)
        pltpu.make_async_copy(held, held, send_sem.at[k, e, g]).wait()

    ring = range(1, SIDE)

    def plain(g):
        return pl.ds(*CUTS[g])

    def right(g):
        return pl.ds(half + CUTS[g][0], CUTS[g][1])

    def gather_first(k, e, g, buf):
        a, b = plain(g), right(g)
        for d in ring:
            send((k, e, g), buf.at[k, y, x, :, a], buf.at[k, y, x, :, a], device("x", d))
            send((k, e, g), buf.at[k, y, x, :, b], buf.at[k, y, x, :, b], device("y", d))

    def gather_second(k, e, g, buf):
        arrive(k, e - 1, g)
        a, b = plain(g), right(g)
        for d in ring:
            send((k, e, g), buf.at[k, y, :, :, a], buf.at[k, y, :, :, a], device("y", d))
            send((k, e, g), buf.at[k, :, x, :, b], buf.at[k, :, x, :, b], device("x", d))

    def scatter_first(k, e, g, i, src, weight, flipped, buf):
        a, b = plain(g), right(g)
        to_features(k, src, weight, flipped, buf, a)
        for d in ring:
            there = big.at[i, k, 0, d - 1, :, :, a]
            send((k, e, g), buf.at[k, at("y", d), :, :, a], there, device("y", d))
        to_features(k, src, weight, flipped, buf, b)
        for d in ring:
            there = big.at[i, k, 1, d - 1, :, :, a]
            send((k, e, g), buf.at[k, :, at("x", d), :, b], there, device("x", d))

    def scatter_second(k, e, g, i, buf):
        arrive(k, e - 1, g)
        a, b = plain(g), right(g)
        for n in range(SIDE):
            total = buf[k, y, n, :, a].astype(F32)
            for d in ring:
                total = total + big[i, k, 0, d - 1, n, :, a].astype(F32)
            sum_a[i, k, n, :, a] = total.astype(BF16)
        for d in ring:
            here = sum_a.at[i, k, at("x", d), :, a]
            send((k, e, g), here, small.at[i, k, 0, d - 1, :, a], device("x", d))
        for n in range(SIDE):
            total = buf[k, n, x, :, b].astype(F32)
            for d in ring:
                total = total + big[i, k, 1, d - 1, n, :, a].astype(F32)
            sum_b[i, k, n, :, a] = total.astype(BF16)
        for d in ring:
            here = sum_b.at[i, k, at("y", d), :, a]
            send((k, e, g), here, small.at[i, k, 1, d - 1, :, a], device("y", d))

    def scatter_total(k, e, g, i):
        arrive(k, e - 1, g)
        cols = plain(g)
        a = sum_a[i, k, x, :, cols].astype(F32)
        b = sum_b[i, k, y, :, cols].astype(F32)
        for d in ring:
            a = a + small[i, k, 0, d - 1, :, cols].astype(F32)
            b = b + small[i, k, 1, d - 1, :, cols].astype(F32)
        return (cols, a), (right(g), b)

    def col_scatter(k, e, g, src, weight, flipped, buf, got):
        cols = plain(g)
        to_units(k, src, weight, flipped, buf, cols)
        for d in ring:
            there = got.at[k, d - 1, :, cols]
            send((k, e, g), buf.at[k, at("z", d), :, cols], there, device("z", d))

    def col_total(k, e, g, buf, got):
        arrive(k, e - 1, g)
        cols = plain(g)
        total = buf[k, z, :, cols].astype(F32)
        for d in ring:
            total = total + got[k, d - 1, :, cols].astype(F32)
        return total

    def col_gather(k, e, g, buf):
        here = buf.at[k, z, :, plain(g)]
        for d in ring:
            send((k, e, g), here, here, device("z", d))

    def times(block, weight, flipped, cols):
        if flipped:
            return lax.dot_general(
                block, weight[cols, :], (((1,), (1,)), ((), ())), preferred_element_type=F32
            ).astype(BF16)
        return jnp.dot(block, weight[:, cols], preferred_element_type=F32).astype(BF16)

    def to_units(k, src, weight, flipped, dst, cols):
        value = times(src[k].reshape(rows, wide), weight, flipped, cols)
        dst[k, :, :, cols] = value.reshape(SIDE, rows // SIDE, cols.size)

    def to_features(k, src, weight, flipped, dst, cols):
        value = times(src[k].reshape(rows, units), weight, flipped, cols)
        dst[k, :, :, :, cols] = value.reshape(SIDE, SIDE, tokens, cols.size)

    def local(k):
        return pl.ds(k * tokens, tokens)

    everyone = CHUNKS * rows

    def weight_gradient(narrow, other_all, result, width):
        def tile(start, size):
            a = narrow[..., pl.ds(start, size)].reshape(everyone, size)
            b = other_all[...].reshape(everyone, width)
            result[pl.ds(start, size), :] = lax.dot_general(
                a, b, (((0,), (0,)), ((), ())), preferred_element_type=F32
            ).astype(BF16)

        return tile

    def event(k, e, g):
        groups = range(len(CUTS))
        if e in (2, 4, 8, 10):
            for other_g in groups:
                arrive(k, e - 1, other_g)
        if e == 0:
            gather_first(k, e, g, x_all)
        elif e == 1:
            gather_second(k, e, g, x_all)
        elif e == 2:
            for g in groups:
                col_scatter(k, e, g, x_all, w1, False, part1, got_z1)
        elif e == 3:
            value, slope = gelu_both(col_total(k, e, g, part1, got_z1))
            hidden_all[k, z, :, plain(g)] = value.astype(BF16)
            col_gather(k, e, g, hidden_all)
            dgelu[k, :, plain(g)] = slope
        elif e == 4:
            for g in groups:
                scatter_first(k, e, g, 0, hidden_all, w2, False, outp)
        elif e == 5:
            scatter_second(k, e, g, 0, outp)
        elif e == 6:
            for cols, total in scatter_total(k, e, g, 0):
                output = (x_ref[local(k), cols].astype(F32) + total).astype(BF16)
                out_ref[local(k), cols] = output
                slope = g_ref[local(k), cols].astype(F32) + feature_weight * (
                    output.astype(F32) - stale[local(k), cols].astype(F32)
                )
                slope_all[k, y, x, :, cols] = slope.astype(BF16)
            gather_first(k, e, g, slope_all)
        elif e == 7:
            gather_second(k, e, g, slope_all)
        elif e == 8:
            for g in groups:
                col_scatter(k, e, g, slope_all, w2, True, part2, got_z2)
        elif e == 9:
            inner = col_total(k, e, g, part2, got_z2) * dgelu[k, :, plain(g)]
            inner_all[k, z, :, plain(g)] = inner.astype(BF16)
            col_gather(k, e, g, inner_all)
        elif e == 10:
            for g in groups:
                scatter_first(k, e, g, 1, inner_all, w1, True, ginp)
        elif e == 11:
            scatter_second(k, e, g, 1, ginp)
        elif e == 12:
            for cols, total in scatter_total(k, e, g, 1):
                mine = slope_all[k, y, x, :, cols].astype(F32)
                gin_ref[local(k), cols] = (mine + total).astype(BF16)
        elif e == 13:
            column_tiles(units, weight_gradient(hidden_all, slope_all, gw2, wide))
            save2.start()
        elif e == 14:
            column_tiles(wide, weight_gradient(x_all, inner_all, gw1, units))
            save1.start()

    swap = pltpu.make_async_remote_copy(
        src_ref=s_ref, dst_ref=stale, send_sem=stale_sem.at[0], recv_sem=stale_sem.at[1],
        device_id=other, device_id_type=MESH,
    )
    save1 = pltpu.make_async_copy(gw1, gw1_ref, out_sem.at[0])
    save2 = pltpu.make_async_copy(gw2, gw2_ref, out_sem.at[1])

    once = {1: swap.start, 2: load1.wait, 4: load2.wait, 6: swap.wait_recv}
    for k, e, g in ORDER:
        if e in once:
            once.pop(e)()
        event(k, e, g)
    swap.wait_send()
    for k in range(CHUNKS):
        for e in range(STEPS):
            for g in range(len(CUTS)):
                leave(k, e, g)
    save2.wait()
    save1.wait()


def body(block_in, weight_in, weight_out, upstream, stale_out):
    x, w1, w2, g, s = block_in[0], weight_in[0], weight_out[0], upstream[0], stale_out[0]
    wide, units = w1.shape
    own = x.shape[0]
    tokens = own // CHUNKS
    rows = tokens * SIDE * SIDE
    half = wide // 2
    share = rows // SIDE
    ring = SIDE - 1
    inside = pl.BlockSpec(memory_space=pltpu.VMEM)
    anywhere = pl.BlockSpec(memory_space=pl.ANY)
    row_all = pltpu.VMEM((CHUNKS, SIDE, SIDE, tokens, wide), BF16)
    col_all = pltpu.VMEM((CHUNKS, SIDE, share, units), BF16)
    col_got = pltpu.VMEM((CHUNKS, ring, share, units), BF16)
    flops = 12 * own * 16 * wide * units
    out, gin, gw1, gw2 = pl.pallas_call(
        kernel,
        out_shape=(
            jax.ShapeDtypeStruct(x.shape, BF16),
            jax.ShapeDtypeStruct(x.shape, BF16),
            jax.ShapeDtypeStruct(w1.shape, BF16),
            jax.ShapeDtypeStruct(w2.shape, BF16),
        ),
        in_specs=[inside, inside, inside, anywhere, anywhere],
        out_specs=(inside, inside, anywhere, anywhere),
        scratch_shapes=[
            pltpu.VMEM((wide, units), BF16),
            pltpu.VMEM((units, wide), BF16),
            pltpu.VMEM(x.shape, BF16),
            row_all,
            row_all,
            col_all,
            col_all,
            pltpu.VMEM((CHUNKS, share, units), F32),
            col_all,
            col_all,
            col_got,
            col_got,
            row_all,
            row_all,
            pltpu.VMEM((2, CHUNKS, 2, ring, SIDE, tokens, half), BF16),
            pltpu.VMEM((2, CHUNKS, 2, ring, tokens, half), BF16),
            pltpu.VMEM((2, CHUNKS, SIDE, tokens, half), BF16),
            pltpu.VMEM((2, CHUNKS, SIDE, tokens, half), BF16),
            pltpu.VMEM((wide, units), BF16),
            pltpu.VMEM((units, wide), BF16),
            pltpu.SemaphoreType.DMA((CHUNKS, STEPS, len(CUTS))),
            pltpu.SemaphoreType.DMA((CHUNKS, STEPS, len(CUTS))),
            pltpu.SemaphoreType.DMA((2,)),
            pltpu.SemaphoreType.DMA((2,)),
            pltpu.SemaphoreType.DMA((2,)),
        ],
        compiler_params=pltpu.CompilerParams(
            collective_id=0, has_side_effects=True, vmem_limit_bytes=60 << 20
        ),
        cost_estimate=pl.CostEstimate(
            flops=flops, bytes_accessed=8 * wide * units, transcendentals=0
        ),
    )(x, g, s, w1, w2)
    return out[None], gin[None], gw1[None], gw2[None]


def solution(mesh):
    placed = (
        P("peer", "row", "col"),
        P("peer", "col", "row"),
        P("peer", "row", "col"),
        P("peer", "row", "col"),
        P("peer", "row", "col"),
    )
    return jax.shard_map(
        body,
        mesh=mesh,
        in_specs=placed,
        out_specs=(
            P("peer", "row", "col"),
            P("peer", "row", "col"),
            P("peer", "col", "row"),
            P("peer", "row", "col"),
        ),
        check_vma=False,
    )
```

time: 139 us -> 120 us (0.86)
  Pallas kernels: 129 us -> 110 us
    pallas_call x1, Pallas kernels: 129 us -> 110 us  [body(): pl.pallas_call(kernel, out_shape=(jax.ShapeDtypeStruct(x.shape, BF16), ja...]
where the time goes in v2:
time: 120 us; the launch traced here: 119 us
  Pallas kernels  110 us (92%)
  local copies, waits for them, and re-layouts  8.88 us (7%)
    pallas_call x1, Pallas kernels, body(): pl.pallas_call(kernel, out_shape=(jax.ShapeDtypeStruct(x.shape, BF16), ja...  110 us
    unnamed x6, local copies, waits for them, and re-layouts  8.88 us

profile of v2, /device:TPU:0, one launch (start us, length us, event | category | flops | bytes accessed | tf_op | source)
XLA Modules:
  0.0 119.5 jit_solution(14649300778928560649)
XLA Ops:
  0.6 109.9 %shard_map.84 = (bf16[48,1792]{1,0:T(8,128)(2,1)}, bf16[48,1792]{1,0:T(8,128)(2,1)}, bf16[1792,896]{1,0:T(8,128)(2,1)}, bf16[896,1792]{1,0:T(8,128)(2,1)}) custom-call(bf16[48,1792]{1,0:T(8,128)(2,1)} %bitcast.15, bf16[48,1792]{1,0:T(8,128)(2,1)} %bitcast.16, bf16[48,1792]{1,0:T(8,128)(2,1)} %bitcast.17, bf16[1792,896]{1,0:T(8,128)(2,1)} %bitcast.13, ...), custom_call_target="tpu_custom_call" | custom-call | flops 14797504512 | bytes 12845056 | tf_op jit(solution)/shard_map/pallas_call | solution.py:328
  110.6 1.6 %copy.13 = bf16[1,48,1792]{2,1,0:T(8,128)(2,1)} copy(bf16[1,48,1792]{2,1,0:T(8,128)(2,1)} %bitcast.12) | data formatting | bytes 344064
  112.2 1.6 %copy.14 = bf16[1,48,1792]{2,1,0:T(8,128)(2,1)} copy(bf16[1,48,1792]{2,1,0:T(8,128)(2,1)} %bitcast.11) | data formatting | bytes 344064
  113.8 0.0 copy-start
  113.8 4.0 %copy.15 = bf16[1,1792,896]{2,1,0:T(8,128)(2,1)} copy(bf16[1,1792,896]{2,1,0:T(8,128)(2,1)} %bitcast.10) | data formatting | bytes 6422528
  117.8 0.0 copy-done
  117.8 1.7 %copy.16 = bf16[1,896,1792]{2,1,0:T(8,128)(2,1)} copy(bf16[1,896,1792]{2,1,0:T(8,128)(2,1)S(1)} %bitcast.9) | data formatting | bytes 6422528
Async XLA Ops:
  113.8 4.0 %copy-start = (bf16[896,1792]{1,0:T(8,128)(2,1)S(1)}, bf16[896,1792]{1,0:T(8,128)(2,1)}, u32[]{:S(2)}) copy-start(bf16[896,1792]{1,0:T(8,128)(2,1)} %get-tuple-element.11) | copy-start | bytes 9633796

commit v3 on v2

--- a/solution.py
+++ b/solution.py
@@ -54,8 +54,8 @@
     out_ref, gin_ref, gw1_ref, gw2_ref,
     w1, w2, stale, x_all, slope_all, hidden_all, inner_all, dgelu,
     part1, part2, got_z1, got_z2, outp, ginp,
-    big, small, sum_a, sum_b, gw1, gw2,
-    send_sem, recv_sem, stale_sem, local_sem, out_sem,
+    big, small, sum_a, sum_b,
+    send_sem, recv_sem, stale_sem, local_sem,
 ):
     tokens = x_ref.shape[0] // CHUNKS
     wide, units = w1.shape
@@ -283,19 +283,14 @@
                 mine = slope_all[k, y, x, :, cols].astype(F32)
                 gin_ref[local(k), cols] = (mine + total).astype(BF16)
         elif e == 13:
-            column_tiles(units, weight_gradient(hidden_all, slope_all, gw2, wide))
-            save2.start()
+            column_tiles(units, weight_gradient(hidden_all, slope_all, gw2_ref, wide))
         elif e == 14:
-            column_tiles(wide, weight_gradient(x_all, inner_all, gw1, units))
-            save1.start()
+            column_tiles(wide, weight_gradient(x_all, inner_all, gw1_ref, units))
 
     swap = pltpu.make_async_remote_copy(
         src_ref=s_ref, dst_ref=stale, send_sem=stale_sem.at[0], recv_sem=stale_sem.at[1],
         device_id=other, device_id_type=MESH,
     )
-    save1 = pltpu.make_async_copy(gw1, gw1_ref, out_sem.at[0])
-    save2 = pltpu.make_async_copy(gw2, gw2_ref, out_sem.at[1])
-
     once = {1: swap.start, 2: load1.wait, 4: load2.wait, 6: swap.wait_recv}
     for k, e, g in ORDER:
         if e in once:
@@ -306,8 +301,6 @@
         for e in range(STEPS):
             for g in range(len(CUTS)):
                 leave(k, e, g)
-    save2.wait()
-    save1.wait()
 
 
 def body(block_in, weight_in, weight_out, upstream, stale_out):
@@ -334,7 +327,7 @@
             jax.ShapeDtypeStruct(w2.shape, BF16),
         ),
         in_specs=[inside, inside, inside, anywhere, anywhere],
-        out_specs=(inside, inside, anywhere, anywhere),
+        out_specs=(inside,) * 4,
         scratch_shapes=[
             pltpu.VMEM((wide, units), BF16),
             pltpu.VMEM((units, wide), BF16),
@@ -354,16 +347,13 @@
             pltpu.VMEM((2, CHUNKS, 2, ring, tokens, half), BF16),
             pltpu.VMEM((2, CHUNKS, SIDE, tokens, half), BF16),
             pltpu.VMEM((2, CHUNKS, SIDE, tokens, half), BF16),
-            pltpu.VMEM((wide, units), BF16),
-            pltpu.VMEM((units, wide), BF16),
             pltpu.SemaphoreType.DMA((CHUNKS, STEPS, len(CUTS))),
             pltpu.SemaphoreType.DMA((CHUNKS, STEPS, len(CUTS))),
             pltpu.SemaphoreType.DMA((2,)),
             pltpu.SemaphoreType.DMA((2,)),
-            pltpu.SemaphoreType.DMA((2,)),
         ],
         compiler_params=pltpu.CompilerParams(
-            collective_id=0, has_side_effects=True, vmem_limit_bytes=60 << 20
+            collective_id=0, has_side_effects=True, vmem_limit_bytes=44 << 20
         ),
         cost_estimate=pl.CostEstimate(
             flops=flops, bytes_accessed=8 * wide * units, transcendentals=0

time: 120 us -> 116 us (0.967)
  Pallas kernels: 110 us -> 108 us
  local copies, waits for them, and re-layouts: 8.88 us -> 7.46 us
    pallas_call x1, Pallas kernels: 110 us -> 108 us  [body(): pl.pallas_call(kernel, out_shape=(jax.ShapeDtypeStruct(x.shape, BF16), ja...]
    unnamed x6 -> x10, local copies, waits for them, and re-layouts: 8.88 us -> 7.46 us
where the time goes in v3:
time: 116 us
  Pallas kernels  108 us (93%)
  local copies, waits for them, and re-layouts  7.46 us (6%)
    pallas_call x1, Pallas kernels, body(): pl.pallas_call(kernel, out_shape=(jax.ShapeDtypeStruct(x.shape, BF16), ja...  108 us
    unnamed x10, local copies, waits for them, and re-layouts  7.46 us

profile of v3, /device:TPU:0, one launch (start us, length us, event | category | flops | bytes accessed | tf_op | source)
XLA Modules:
  0.0 116.2 jit_solution(14951878874675330375)
XLA Ops:
  0.6 0.0 copy-start
  0.6 0.9 copy-done
  1.6 0.0 copy-start.1
  1.6 0.9 copy-done.1
  2.5 0.0 copy-start.2
  2.5 0.9 copy-done.2
  3.4 108.1 %shard_map.84 = (bf16[48,1792]{1,0:T(8,128)(2,1)S(1)}, bf16[48,1792]{1,0:T(8,128)(2,1)S(1)}, bf16[1792,896]{1,0:T(8,128)(2,1)S(1)}, bf16[896,1792]{1,0:T(8,128)(2,1)S(1)}) custom-call(bf16[48,1792]{1,0:T(8,128)(2,1)S(1)} %bitcast.13, bf16[48,1792]{1,0:T(8,128)(2,1)S(1)} %bitcast.14, bf16[48,1792]{1,0:T(8,128)(2,1)S(1)} %bitcast.15, ...), custom_call_target="tpu_custom_call" | custom-call | flops 14797504512 | bytes 12845056 | tf_op jit(solution)/shard_map/pallas_call | solution.py:321
  111.5 0.7 copy.13
  112.2 0.7 copy.14
  112.9 1.7 %copy.15 = bf16[1,1792,896]{2,1,0:T(8,128)(2,1)} copy(bf16[1,1792,896]{2,1,0:T(8,128)(2,1)S(1)} %bitcast.10) | data formatting | bytes 6422528
  114.5 1.7 %copy.16 = bf16[1,896,1792]{2,1,0:T(8,128)(2,1)} copy(bf16[1,896,1792]{2,1,0:T(8,128)(2,1)S(1)} %bitcast.9) | data formatting | bytes 6422528
Async XLA Ops:
  0.6 0.9 copy-start
  1.6 0.9 copy-start.1
  2.5 0.9 copy-start.2

commit v4 on v3

--- a/solution.py
+++ b/solution.py
@@ -13,15 +13,15 @@
 CUTS = ((0, 512), (512, 384))
 STEPS = 12
 ORDER = (
-    (0, 0, 1), (0, 0, 0), (1, 0, 1), (0, 1, 1), (1, 0, 0), (0, 1, 0), (1, 1, 0), (1, 1, 1),
-    (0, 2, 0), (2, 0, 0), (2, 0, 1), (1, 2, 0), (2, 1, 1), (2, 1, 0), (0, 3, 1), (0, 3, 0),
-    (1, 3, 1), (1, 3, 0), (0, 4, 0), (2, 2, 0), (1, 4, 0), (0, 5, 1), (2, 3, 1), (0, 5, 0),
-    (1, 5, 0), (0, 6, 1), (0, 6, 0), (2, 3, 0), (1, 5, 1), (0, 7, 1), (0, 7, 0), (2, 4, 0),
-    (0, 8, 0), (1, 6, 0), (1, 6, 1), (2, 5, 0), (2, 5, 1), (1, 7, 0), (0, 9, 0), (2, 6, 0),
-    (1, 7, 1), (0, 9, 1), (2, 6, 1), (2, 7, 0), (2, 7, 1), (1, 8, 0), (0, 10, 0), (2, 8, 0),
-    (1, 9, 0), (1, 9, 1), (0, 13, 0), (0, 11, 1), (0, 11, 0), (2, 9, 0), (2, 9, 1), (1, 10, 0),
-    (0, 12, 0), (2, 10, 0), (0, 14, 0), (1, 11, 0), (1, 11, 1), (2, 11, 0), (2, 11, 1), (0, 12, 1),
-    (2, 12, 0), (1, 12, 0), (1, 12, 1), (2, 12, 1),
+    (0, 0, 1), (1, 0, 0), (1, 0, 1), (0, 0, 0), (2, 0, 0), (0, 1, 1), (0, 1, 0), (0, 2, 0),
+    (2, 0, 1), (1, 1, 1), (2, 1, 0), (1, 1, 0), (0, 3, 0), (0, 3, 1), (1, 2, 0), (2, 1, 1),
+    (0, 4, 0), (1, 3, 0), (1, 3, 1), (0, 5, 0), (2, 2, 0), (0, 5, 1), (0, 6, 0), (1, 4, 0),
+    (0, 6, 1), (2, 3, 0), (0, 7, 0), (2, 3, 1), (0, 7, 1), (1, 5, 0), (1, 5, 1), (2, 4, 0),
+    (0, 8, 0), (1, 6, 0), (2, 5, 0), (1, 6, 1), (1, 7, 0), (2, 5, 1), (0, 9, 1), (2, 6, 0),
+    (0, 9, 0), (1, 7, 1), (2, 6, 1), (2, 7, 0), (2, 7, 1), (1, 8, 0), (0, 10, 0), (2, 8, 0),
+    (0, 11, 0), (1, 9, 0), (1, 9, 1), (0, 13, 1), (0, 13, 0), (0, 11, 1), (2, 9, 1), (2, 9, 0),
+    (1, 10, 0), (2, 10, 0), (0, 14, 1), (0, 14, 0), (1, 11, 1), (0, 14, 2), (1, 11, 0), (2, 11, 0),
+    (2, 11, 1), (1, 12, 1), (0, 12, 0), (0, 14, 3), (2, 12, 0), (1, 12, 0), (0, 12, 1), (2, 12, 1),
 )
 MESH = pl.DeviceIdType.MESH
 F32 = jnp.float32
@@ -37,16 +37,9 @@
     return value, slope
 
 
-def column_tiles(width, run):
-    full = width // 256
-
-    def step(n, carry):
-        run(pl.multiple_of(n * 256, 256), 256)
-        return carry
-
-    lax.fori_loop(0, full, step, 0)
-    if width % 256:
-        run(full * 256, width % 256)
+def column_tiles(part, width, run):
+    for start in range(part * 512, min(width, part * 512 + 512), 256):
+        run(start, min(256, width - start))
 
 
 def kernel(
@@ -283,9 +276,9 @@
                 mine = slope_all[k, y, x, :, cols].astype(F32)
                 gin_ref[local(k), cols] = (mine + total).astype(BF16)
         elif e == 13:
-            column_tiles(units, weight_gradient(hidden_all, slope_all, gw2_ref, wide))
+            column_tiles(g, units, weight_gradient(hidden_all, slope_all, gw2_ref, wide))
         elif e == 14:
-            column_tiles(wide, weight_gradient(x_all, inner_all, gw1_ref, units))
+            column_tiles(g, wide, weight_gradient(x_all, inner_all, gw1_ref, units))
 
     swap = pltpu.make_async_remote_copy(
         src_ref=s_ref, dst_ref=stale, send_sem=stale_sem.at[0], recv_sem=stale_sem.at[1],

time: 116 us -> 112 us (0.966)
  Pallas kernels: 108 us -> 104 us
    pallas_call x1, Pallas kernels: 108 us -> 104 us  [body(): pl.pallas_call(kernel, out_shape=(jax.ShapeDtypeStruct(x.shape, BF16), ja...]
where the time goes in v4:
time: 112 us
  Pallas kernels  104 us (93%)
  local copies, waits for them, and re-layouts  7.46 us (7%)
    pallas_call x1, Pallas kernels, body(): pl.pallas_call(kernel, out_shape=(jax.ShapeDtypeStruct(x.shape, BF16), ja...  104 us
    unnamed x10, local copies, waits for them, and re-layouts  7.46 us

profile of v4, /device:TPU:0, one launch (start us, length us, event | category | flops | bytes accessed | tf_op | source)
XLA Modules:
  0.0 111.9 jit_solution(15768167591775302469)
XLA Ops:
  0.6 0.0 copy-start
  0.6 0.9 copy-done
  1.6 0.0 copy-start.1
  1.6 0.9 copy-done.1
  2.5 0.0 copy-start.2
  2.5 0.9 copy-done.2
  3.4 103.8 %shard_map.84 = (bf16[48,1792]{1,0:T(8,128)(2,1)S(1)}, bf16[48,1792]{1,0:T(8,128)(2,1)S(1)}, bf16[1792,896]{1,0:T(8,128)(2,1)S(1)}, bf16[896,1792]{1,0:T(8,128)(2,1)S(1)}) custom-call(bf16[48,1792]{1,0:T(8,128)(2,1)S(1)} %bitcast.13, bf16[48,1792]{1,0:T(8,128)(2,1)S(1)} %bitcast.14, bf16[48,1792]{1,0:T(8,128)(2,1)S(1)} %bitcast.15, ...), custom_call_target="tpu_custom_call" | custom-call | flops 14797504512 | bytes 12845056 | tf_op jit(solution)/shard_map/pallas_call | solution.py:314
  107.2 0.7 copy.13
  107.9 0.7 copy.14
  108.6 1.7 %copy.15 = bf16[1,1792,896]{2,1,0:T(8,128)(2,1)} copy(bf16[1,1792,896]{2,1,0:T(8,128)(2,1)S(1)} %bitcast.10) | data formatting | bytes 6422528
  110.3 1.7 %copy.16 = bf16[1,896,1792]{2,1,0:T(8,128)(2,1)} copy(bf16[1,896,1792]{2,1,0:T(8,128)(2,1)S(1)} %bitcast.9) | data formatting | bytes 6422528
Async XLA Ops:
  0.6 0.9 copy-start
  1.6 0.9 copy-start.1
  2.5 0.9 copy-start.2

commit v5 on v4

--- a/solution.py
+++ b/solution.py
@@ -10,7 +10,7 @@
 feature_weight = 1.0
 SIDE = 4
 CHUNKS = 3
-CUTS = ((0, 512), (512, 384))
+CUTS = ((0, 384), (384, 512))
 STEPS = 12
 ORDER = (
     (0, 0, 1), (1, 0, 0), (1, 0, 1), (0, 0, 0), (2, 0, 0), (0, 1, 1), (0, 1, 0), (0, 2, 0),

time: 112 us -> 112 us (level)
  no operation moved by 1% of the time
where the time goes in v5:
time: 112 us
  Pallas kernels  104 us (93%)
  local copies, waits for them, and re-layouts  7.46 us (7%)
    pallas_call x1, Pallas kernels, body(): pl.pallas_call(kernel, out_shape=(jax.ShapeDtypeStruct(x.shape, BF16), ja...  104 us
    unnamed x10, local copies, waits for them, and re-layouts  7.46 us

profile of v5, /device:TPU:0, one launch (start us, length us, event | category | flops | bytes accessed | tf_op | source)
XLA Modules:
  0.0 111.7 jit_solution(15299744971355870910)
XLA Ops:
  0.6 0.0 copy-start
  0.6 0.9 copy-done
  1.6 0.0 copy-start.1
  1.6 0.9 copy-done.1
  2.5 0.0 copy-start.2
  2.5 0.9 copy-done.2
  3.4 103.6 %shard_map.84 = (bf16[48,1792]{1,0:T(8,128)(2,1)S(1)}, bf16[48,1792]{1,0:T(8,128)(2,1)S(1)}, bf16[1792,896]{1,0:T(8,128)(2,1)S(1)}, bf16[896,1792]{1,0:T(8,128)(2,1)S(1)}) custom-call(bf16[48,1792]{1,0:T(8,128)(2,1)S(1)} %bitcast.13, bf16[48,1792]{1,0:T(8,128)(2,1)S(1)} %bitcast.14, bf16[48,1792]{1,0:T(8,128)(2,1)S(1)} %bitcast.15, ...), custom_call_target="tpu_custom_call" | custom-call | flops 14797504512 | bytes 12845056 | tf_op jit(solution)/shard_map/pallas_call | solution.py:314
  107.0 0.7 copy.13
  107.6 0.7 copy.14
  108.3 1.7 %copy.15 = bf16[1,1792,896]{2,1,0:T(8,128)(2,1)} copy(bf16[1,1792,896]{2,1,0:T(8,128)(2,1)S(1)} %bitcast.10) | data formatting | bytes 6422528
  110.0 1.7 %copy.16 = bf16[1,896,1792]{2,1,0:T(8,128)(2,1)} copy(bf16[1,896,1792]{2,1,0:T(8,128)(2,1)S(1)} %bitcast.9) | data formatting | bytes 6422528
Async XLA Ops:
  0.6 0.9 copy-start
  1.6 0.9 copy-start.1
  2.5 0.9 copy-start.2
